TPU v7x, 32 devices: a whole 2x2x4 slice. The times are simulated.
32 devices in a mesh: groups: 2 (over y), people: 4 (over z), blocks: 2 (over x), sub: 2 (over core).
Axes of the slice: x: 2, y: 2, z: 4, core: 2. Of those that a mesh axis runs over, the one named last changes fastest.
Arguments:
- dosage: int32 [4096, 2048], P(('groups', 'people', 'sub'), 'blocks'), parts along dimension 0, may hold values from 0 to 200
- fold: int32 [4096], P(('groups', 'people', 'sub')), parts along dimension 0, may hold values from 0 to 1, as said below
- pheno: bfloat16 [4096, 48], P(('groups', 'people', 'sub')), parts along dimension 0, may hold values from -8 to 8
- ridges: float32 [5], replicated, may hold values from 1 to 20
Outputs:
- second: float32 [48, 5, 4096], P(('blocks', 'sub'), None, ('groups', 'people')), parts along dimension 2
There are 2 independent parts, one for each index of `groups`. A program takes and returns all parts, laid end to end along the dimension named above; an argument that names none is the same for every part. Nothing has to cross between parts.
Inputs may be any that keep to these rules, and one draw needn't show every extreme that they name: Each fold holds exactly 1024 people.
All inputs are finite; a program needn't handle non-finite values.
Results may differ from a plain program's by a relative error of at most 0.0021.
Values may be sent and summed in bfloat16 or wider, within the bound.
A program may use at most 64 MiB of HBM per device.

v0:
```python
import jax
import jax.numpy as jnp
from jax import lax
from jax.sharding import PartitionSpec as P

TRAITS = 48
RIDGES = 5
FOLDS = 2
ITERS = 10
ITERS_TWO = 4


highest = lax.Precision.HIGHEST


def conjugate(apply_system, right_side, steps):
    estimate = jnp.zeros_like(right_side)
    residual = right_side
    direction = right_side
    current = jnp.sum(residual * residual, -2, keepdims=True)
    for step in range(steps):
        image = apply_system(direction)
        alpha = current / jnp.sum(direction * image, -2, keepdims=True)
        estimate = estimate + alpha * direction
        residual = residual - alpha * image
        following = jnp.sum(residual * residual, -2, keepdims=True)
        direction = residual + following / current * direction
        current = following
    return estimate


def covariance_rows(gram_rows, row_sums, all_sums, row_mean, all_mean, train_count):
    return (
        gram_rows
        - row_sums[:, None] * all_mean[None, :]
        - row_mean[:, None] * all_sums[None, :]
        + train_count * row_mean[:, None] * all_mean[None, :]
    )


def train_total(pieces, fold_index):
    return sum([pieces[other] for other in range(FOLDS) if other != fold_index])


def system_rows(shares, sums_all, column_mean, column_spread, row_start, share_rows, train_count):
    row_mean = lax.dynamic_slice_in_dim(column_mean, row_start, share_rows, 0)
    row_spread = lax.dynamic_slice_in_dim(column_spread, row_start, share_rows, 0)
    systems = []
    for fold_index in range(FOLDS):
        sums_train = train_total(sums_all, fold_index)
        row_sums = lax.dynamic_slice_in_dim(sums_train, row_start, share_rows, 0)
        covariance = covariance_rows(
            train_total(shares, fold_index),
            row_sums,
            sums_train,
            row_mean,
            column_mean,
            train_count,
        )
        systems.append(covariance / (train_count * row_spread[:, None] * column_spread[None, :]))
    return (jnp.stack(systems), row_spread)


def shards(dosage, fold, pheno, ridges):
    row_count, block_size = dosage.shape
    people_count = lax.axis_size("people")
    sub_count = lax.axis_size("sub")
    people = row_count * people_count * sub_count
    train_count = people - people // FOLDS
    centred = (dosage - 100).astype(jnp.bfloat16)
    pheno_wide = pheno.astype(jnp.float32)
    masks = [fold[:, None] == fold_index for fold_index in range(FOLDS)]
    grams, sums, squares, cross, totals = ([], [], [], [], [])
    for mask in masks:
        masked = jnp.where(mask, centred, jnp.zeros_like(centred))
        grams.append(
            lax.dot_general(
                masked, centred, (((0,), (0,)), ((), ())), preferred_element_type=jnp.float32
            )
        )
        masked_wide = masked.astype(jnp.float32)
        sums.append(jnp.sum(masked_wide, 0))
        squares.append(jnp.sum(masked_wide * masked_wide, 0))
        cross.append(
            lax.dot_general(
                masked, pheno, (((0,), (0,)), ((), ())), preferred_element_type=jnp.float32
            )
        )
        totals.append(jnp.sum(jnp.where(mask, pheno_wide, 0.0), 0))
    sums_all, squares_all, cross_all, totals_all = lax.psum(
        (jnp.stack(sums), jnp.stack(squares), jnp.stack(cross), jnp.stack(totals)),
        ("people", "sub"),
    )
    column_mean = sum([sums_all[fold_index] for fold_index in range(FOLDS)]) / people
    column_spread = jnp.sqrt(
        sum([squares_all[fold_index] for fold_index in range(FOLDS)]) / people
        - column_mean * column_mean
        + 1e-05
    )
    right_sides = []
    for fold_index in range(FOLDS):
        right_sides.append(
            (
                train_total(cross_all, fold_index)
                - column_mean[:, None] * train_total(totals_all, fold_index)[None, :]
            )
            / (train_count * column_spread[:, None])
        )
    gram_stack = jnp.stack(grams)
    share_rows = block_size // (people_count * sub_count)
    row_start = (lax.axis_index("people") * sub_count + lax.axis_index("sub")) * share_rows
    shares = lax.psum_scatter(gram_stack, ("people", "sub"), scatter_dimension=1, tiled=True)
    systems, row_spread = system_rows(
        shares, sums_all, column_mean, column_spread, row_start, share_rows, train_count
    )
    whole = lax.all_gather(systems, ("people", "sub"), axis=1, tiled=True)
    own_fold = lax.axis_index("sub")
    system = lax.dynamic_index_in_dim(whole, own_fold, 0, keepdims=False)
    trait_share = TRAITS // people_count
    trait_start = lax.axis_index("people") * trait_share
    right_own = lax.dynamic_index_in_dim(jnp.stack(right_sides), own_fold, 0, keepdims=False)
    right_cols = lax.dynamic_slice_in_dim(right_own, trait_start, trait_share, 1)
    shifts = jnp.repeat(ridges, trait_share)
    estimate = conjugate(
        lambda direction: jnp.dot(system, direction, precision=highest) + shifts * direction,
        jnp.tile(right_cols, (1, RIDGES)),
        ITERS,
    )
    scaled = (estimate / column_spread[:, None]).astype(jnp.bfloat16)
    scaled = scaled.reshape(block_size, RIDGES, trait_share)
    gathered = lax.all_gather(scaled[None], ("people", "sub"), axis=0, tiled=True)
    coefficients = gathered.reshape(people_count, sub_count, block_size, RIDGES, trait_share)
    coefficients = coefficients.transpose(1, 2, 3, 0, 4).reshape(FOLDS, block_size, RIDGES * TRAITS)
    prediction = jnp.zeros((row_count, RIDGES * TRAITS), jnp.float32)
    for fold_index in range(FOLDS):
        offset = jnp.dot(
            column_mean, coefficients[fold_index].astype(jnp.float32), precision=highest
        )
        outcome = (
            jnp.dot(centred, coefficients[fold_index], preferred_element_type=jnp.float32) - offset
        )
        prediction = prediction + jnp.where(masks[fold_index], outcome, 0.0)
    prediction = prediction.astype(jnp.bfloat16).reshape(1, row_count, RIDGES, TRAITS)
    moved, moved_pheno = (
        lax.all_to_all(prediction, ("blocks", "sub"), split_axis=3, concat_axis=0, tiled=True),
        lax.all_to_all(
            pheno[None, :, None, :], ("blocks", "sub"), split_axis=3, concat_axis=0, tiled=True
        ),
    )
    block_count = lax.axis_size("blocks")
    trait_group = TRAITS // (block_count * sub_count)
    predictors = moved.reshape(block_count, sub_count, row_count, RIDGES, trait_group)
    predictors = predictors.transpose(1, 2, 4, 0, 3).reshape(
        sub_count * row_count, trait_group, block_count * RIDGES
    )
    targets = moved_pheno.reshape(block_count, sub_count, row_count, trait_group)[0]
    targets = targets.reshape(sub_count * row_count, trait_group)
    gram_two = jnp.einsum(
        "nta,ntb->tab", predictors, predictors, preferred_element_type=jnp.float32
    )
    cross_two = jnp.einsum("nt,nta->ta", targets, predictors, preferred_element_type=jnp.float32)
    gram_two, cross_two = lax.psum((gram_two, cross_two), "people")
    gram_two = gram_two / people
    cross_two = cross_two / people
    predictor_count = block_count * RIDGES
    level = jnp.trace(gram_two, axis1=1, axis2=2) / predictor_count + 1e-06
    level_shift = ridges[None, None, :] * level[:, None, None]
    right_two = jnp.broadcast_to(cross_two[:, :, None], (trait_group, predictor_count, RIDGES))
    weights = conjugate(
        lambda direction: jnp.einsum("tab,tbr->tar", gram_two, direction, precision=highest)
        + level_shift * direction,
        right_two,
        ITERS_TWO,
    )
    return jnp.einsum("nta,tar->trn", predictors.astype(jnp.float32), weights, precision=highest)


def solution(mesh):
    return jax.shard_map(
        shards,
        mesh=mesh,
        in_specs=(
            P(("groups", "people", "sub"), "blocks"),
            P(("groups", "people", "sub")),
            P(("groups", "people", "sub"), None),
            P(),
        ),
        out_specs=P(("blocks", "sub"), None, ("groups", "people")),
        check_vma=False,
    )
```

profile of v0, /device:TPU:0, one launch (start us, length us, event | category | flops | bytes accessed | tf_op | source)
XLA Modules:
  0.0 376.5 jit_solution(10997729040896676900)
XLA Ops:
  6.5 0.7 broadcast_compare_fusion
  7.2 1.7 convert_reduce_fusion.1
  8.9 0.8 convolution_bitcast_fusion
  9.7 0.8 convolution_bitcast_fusion.1
  10.6 4.1 %pad_maximum_fusion = f32[2,1024,1024]{2,1,0:T(8,128)} fusion(f32[1,1024,1024]{2,1,0:T(8,128)S(1)} %convolution_bitcast_fusion, f32[1,1024,1024]{2,1,0:T(8,128)S(1)} %convolution_bitcast_fusion.1), kind=kLoop, calls=%fused_computation | loop fusion | flops 2097152 | bytes 16777216 | tf_op jit(solution)/shard_map/stack | solution.py:109
  14.7 0.6 copy-done
  15.9 0.8 pad_maximum_fusion.2
  17.0 31.6 %all-reduce = (f32[2,1024]{1,0:T(2,128)S(1)}, f32[2,1024]{1,0:T(2,128)S(1)}, f32[2,48]{1,0:T(2,128)S(1)}) all-reduce(f32[2,1024]{1,0:T(2,128)S(1)} %get-tuple-element.88, f32[2,1024]{1,0:T(2,128)S(1)} %get-tuple-element.87, f32[2,48]{1,0:T(2,128)S(1)} %pad_maximum_fusion.5), channel_id=1, replica_groups=mesh['groups'=2,'people'=4,'blocks'=2,'sub'=2] {'people','sub'}, use_global_device_ids=true, to_apply=%region_9.10 | all-reduce | flops 4192 | bytes 33536 | tf_op jit(solution)/shard_map/psum | solution.py:90
  48.8 58.8 %reduce-scatter.2.cloned.1.call-done = f32[2,128,1024]{2,1,0:T(8,128)} async-done(((f32[2,1024,1024]{2,1,0:T(8,128)}), f32[2,128,1024]{2,1,0:T(8,128)}) %reduce-scatter.2.cloned.1.call-update) | async-done | bytes 1048592 | tf_op jit(solution)/shard_map/reduce_scatter | solution.py:112
  107.6 1.7 multiply_divide_fusion.1
  109.3 1.2 pad_maximum_fusion.1
  110.6 0.5 broadcast.463
  111.1 0.8 reduce.4
  111.9 0.6 reshape.722
  112.5 3.4 all-to-all-start.1
  116.1 3.5 all-to-all-done.1
  119.7 44.3 %all-reduce.4.cloned.1.call-done = f32[2,1024,48]{1,2,0:T(8,128)} async-done(((f32[2,1024,48]{1,2,0:T(8,128)}), f32[2,1024,48]{1,2,0:T(8,128)}) %all-reduce.4.cloned.1.call-update) | async-done | bytes 393232 | tf_op jit(solution)/shard_map/psum | solution.py:90
  163.9 1.1 fusion.89
  165.4 81.3 %all-gather.2.cloned.1.call-done = f32[2,1024,1024]{2,1,0:T(8,128)} async-done(((f32[2,128,1024]{2,1,0:T(8,128)}), f32[2,1024,1024]{2,1,0:T(8,128)}) %all-gather.2.cloned.1.call-update) | async-done | bytes 8388624 | tf_op jit(solution)/shard_map/all_gather | solution.py:116
  246.7 6.4 %multiply_reduce_fusion.17 = (f32[60]{0:T(128)S(1)}, f32[1024,60]{0,1:T(8,128)S(1)}) fusion(f32[1024,60]{0,1:T(8,128)S(1)} %tile.16, f32[60]{0:T(128)S(1)} %mul.733, f32[2,1024,1024]{2,1,0:T(8,128)} %all-gather.2.cloned.1.call-done, s32[]{:T(128)S(6)} %select_n.49), kind=kOutput, calls=%fused_computation.123 | convolution fusion | flops 755220416 | bytes 4965108 | tf_op jit(solution)/shard_map/dot_general | solution.py:125
  253.5 6.5 %multiply_reduce_fusion.15 = (f32[60]{0:T(128)S(1)}, f32[1024,60]{0,1:T(8,128)S(1)}) fusion(f32[1024,60]{0,1:T(8,128)S(1)} %multiply_add_fusion.10, f32[60]{0:T(128)S(1)} %mul.733, f32[2,1024,1024]{2,1,0:T(8,128)} %all-gather.2.cloned.1.call-done, s32[]{:T(128)S(6)} %select_n.49), kind=kOutput, calls=%fused_computation.119 | convolution fusion | flops 755220416 | bytes 4965108 | tf_op jit(solution)/shard_map/dot_general | solution.py:125
  260.4 6.5 %multiply_reduce_fusion.13 = (f32[60]{0:T(128)S(1)}, f32[1024,60]{0,1:T(8,128)S(1)}) fusion(f32[1024,60]{0,1:T(8,128)S(1)} %multiply_add_fusion.9, f32[60]{0:T(128)S(1)} %mul.733, f32[2,1024,1024]{2,1,0:T(8,128)} %all-gather.2.cloned.1.call-done, s32[]{:T(128)S(6)} %select_n.49), kind=kOutput, calls=%fused_computation.115 | convolution fusion | flops 755220416 | bytes 4965108 | tf_op jit(solution)/shard_map/dot_general | solution.py:125
  267.2 6.7 %multiply_reduce_fusion.11 = (f32[60]{0:T(128)S(1)}, f32[1024,60]{0,1:T(8,128)S(1)}) fusion(f32[1024,60]{0,1:T(8,128)S(1)} %multiply_add_fusion.8, f32[60]{0:T(128)S(1)} %mul.733, f32[2,1024,1024]{2,1,0:T(8,128)} %all-gather.2.cloned.1.call-done, s32[]{:T(128)S(6)} %select_n.49), kind=kOutput, calls=%fused_computation.111 | convolution fusion | flops 755220416 | bytes 4965108 | tf_op jit(solution)/shard_map/dot_general | solution.py:125
  274.2 6.5 %multiply_reduce_fusion.9 = (f32[60]{0:T(128)S(1)}, f32[1024,60]{0,1:T(8,128)S(1)}) fusion(f32[1024,60]{0,1:T(8,128)S(1)} %multiply_add_fusion.7, f32[60]{0:T(128)S(1)} %mul.733, f32[2,1024,1024]{2,1,0:T(8,128)} %all-gather.2.cloned.1.call-done, s32[]{:T(128)S(6)} %select_n.49), kind=kOutput, calls=%fused_computation.107 | convolution fusion | flops 755220416 | bytes 4965108 | tf_op jit(solution)/shard_map/dot_general | solution.py:125
  281.0 6.5 %multiply_reduce_fusion.7 = (f32[60]{0:T(128)S(1)}, f32[1024,60]{0,1:T(8,128)S(1)}) fusion(f32[1024,60]{0,1:T(8,128)S(1)} %multiply_add_fusion.6, f32[60]{0:T(128)S(1)} %mul.733, f32[2,1024,1024]{2,1,0:T(8,128)} %all-gather.2.cloned.1.call-done, s32[]{:T(128)S(6)} %select_n.49), kind=kOutput, calls=%fused_computation.103 | convolution fusion | flops 755220416 | bytes 4965108 | tf_op jit(solution)/shard_map/dot_general | solution.py:125
  287.8 6.6 %multiply_reduce_fusion.5 = (f32[60]{0:T(128)S(1)}, f32[1024,60]{0,1:T(8,128)S(1)}) fusion(f32[1024,60]{0,1:T(8,128)S(1)} %multiply_add_fusion.5, f32[60]{0:T(128)S(1)} %mul.733, f32[2,1024,1024]{2,1,0:T(8,128)} %all-gather.2.cloned.1.call-done, s32[]{:T(128)S(6)} %select_n.49), kind=kOutput, calls=%fused_computation.99 | convolution fusion | flops 755220416 | bytes 4965108 | tf_op jit(solution)/shard_map/dot_general | solution.py:125
  294.8 7.0 %multiply_reduce_fusion.3 = (f32[60]{0:T(128)S(1)}, f32[1024,60]{0,1:T(8,128)S(1)}) fusion(f32[1024,60]{0,1:T(8,128)S(1)} %multiply_add_fusion.4, f32[60]{0:T(128)S(1)} %mul.733, f32[2,1024,1024]{2,1,0:T(8,128)} %all-gather.2.cloned.1.call-done, s32[]{:T(128)S(6)} %select_n.49), kind=kOutput, calls=%fused_computation.95 | convolution fusion | flops 755220416 | bytes 4965108 | tf_op jit(solution)/shard_map/dot_general | solution.py:125
  302.1 6.5 %multiply_reduce_fusion.1 = (f32[60]{0:T(128)S(1)}, f32[1024,60]{0,1:T(8,128)S(1)}) fusion(f32[1024,60]{0,1:T(8,128)S(1)} %multiply_add_fusion.3, f32[60]{0:T(128)S(1)} %mul.733, f32[2,1024,1024]{2,1,0:T(8,128)} %all-gather.2.cloned.1.call-done, s32[]{:T(128)S(6)} %select_n.49), kind=kOutput, calls=%fused_computation.91 | convolution fusion | flops 755220416 | bytes 4965108 | tf_op jit(solution)/shard_map/dot_general | solution.py:125
  308.9 4.3 %fusion.67 = f32[60]{0:T(128)S(1)} fusion(f32[2,1024,1024]{2,1,0:T(8,128)S(1)} %bitcast.162, s32[]{:T(128)S(6)} %select_n.49, f32[1024,60]{0,1:T(8,128)S(1)} %get-tuple-element.23, f32[1024,60]{0,1:T(8,128)S(1)} %multiply_add_fusion.3, f32[60]{0:T(128)S(1)} %div.291, f32[60]{0:T(128)S(1)} %mul.733), kind=kOutput, calls=%fused_computation.56 | convolution fusion | flops 755466176 | bytes 5244660 | tf_op jit(solution)/shard_map/dot_general | solution.py:125
  313.5 17.6 %all_gather.7 = bf16[8,1024,5,12]{1,3,2,0:T(8,128)(2,1)S(1)} all-gather(bf16[1,1024,5,12]{1,3,2,0:T(8,128)(2,1)S(1)} %broadcast_in_dim_reshape.2), channel_id=1, replica_groups=mesh['groups'=2,'people'=4,'blocks'=2,'sub'=2] {'people','sub'}, dimensions={0}, use_global_device_ids=true | all-gather | bytes 1105920 | tf_op jit(solution)/shard_map/all_gather | solution.py:131
  331.1 1.0 copy.84
  332.2 1.6 fusion.149
  333.8 0.5 copy.54
  334.5 0.5 fusion.124
  334.9 0.6 copy.55
  335.6 0.5 fusion.122
  336.1 0.4 fusion.65
  336.5 0.3 fusion.66
  336.8 0.7 copy.56
  337.5 3.4 all-to-all-start
  341.1 5.1 %all-to-all-done = bf16[1,256,5,48]{1,2,0,3:T(8,128)(2,1)S(1)} async-done(((bf16[1,256,5,48]{1,2,0,3:T(8,128)(2,1)}), bf16[1,256,5,48]{1,2,0,3:T(8,128)(2,1)S(1)}, u32[]{:S(2)}, u32[]{:S(2)}) %all-to-all-start) | async-done | bytes 122912 | tf_op jit(solution)/shard_map/all_to_all | solution.py:145
  346.9 19.0 %all-reduce.1 = (f32[12,10,10]{2,1,0:T(8,128)S(1)}, f32[12,10]{1,0:T(8,128)S(1)}) all-reduce(f32[12,10,10]{2,1,0:T(8,128)S(1)} %fusion.94, f32[12,10]{1,0:T(8,128)S(1)} %bitcast.176), channel_id=1, replica_groups=mesh['groups'=2,'people'=4,'blocks'=2,'sub'=2] {'people'}, use_global_device_ids=true, to_apply=%region_33.34 | all-reduce | flops 1320 | bytes 10560 | tf_op jit(solution)/shard_map/psum | solution.py:162
  366.2 0.4 multiply_reduce_fusion.23
  366.9 0.4 multiply_reduce_fusion.21
  367.7 0.4 multiply_reduce_fusion.19
  368.2 0.4 fusion.71
  368.7 0.3 fusion.90
  369.0 0.7 copy.65
  (101 shorter events, 7.0 us)
Async XLA Ops:
  6.5 101.1 %reduce-scatter.2.cloned.1.call-start = ((), (), s32[]{:S(2)}) async-start(), calls=%async_computation.4 | async-start | bytes 9437184 | tf_op jit(solution)/shard_map/reduce_scatter | solution.py:112
  14.6 0.7 copy-start
  14.7 101.3 %copy-start.1 = (f32[5]{0:T(128)S(1)}, f32[5]{0:T(128)}, u32[]{:S(2)}) copy-start(f32[5]{0:T(128)} %param.7) | copy-start | bytes 64
  14.7 149.3 %all-reduce.4.cloned.1.call-start = ((), (), s32[]{:S(2)}) async-start(), calls=%async_computation.3 | async-start | bytes 786432 | tf_op jit(solution)/shard_map/psum | solution.py:90
  16.7 229.9 %all-gather.2.cloned.1.call-start = ((), (), s32[]{:S(2)}) async-start(), calls=%async_computation.5 | async-start | bytes 9437184 | tf_op jit(solution)/shard_map/all_gather | solution.py:116
  112.5 7.1 %all-to-all-start.1 = ((bf16[4,2,1536]{2,1,0:T(2,128)(2,1)}), bf16[4,2,1536]{2,1,0:T(2,128)(2,1)S(1)}, u32[]{:S(2)}, u32[]{:S(2)}) async-start(bf16[4,2,1536]{2,1,0:T(2,128)(2,1)} %reshape.722), calls=%async_computation.2 | async-start | bytes 49152 | tf_op jit(solution)/shard_map/all_to_all | solution.py:146
  287.8 21.0 %slice-start = ((s8[8388608]{0:T(1024)(128)(4,1)}), s8[4194304]{0:T(1024)(128)(4,1)S(1)}, s32[]{:S(2)}) async-start(s8[8388608]{0:T(1024)(128)(4,1)} %bitcast.161), calls=%async_computation.6 | async-start | bytes 8388608
  294.8 14.1 %slice-start.1 = ((s8[8388608]{0:T(1024)(128)(4,1)}), s8[4194304]{0:T(1024)(128)(4,1)S(1)}, s32[]{:S(2)}) async-start(s8[8388608]{0:T(1024)(128)(4,1)} %bitcast.161), calls=%async_computation.7 | async-start | bytes 8388608
  337.5 8.7 %all-to-all-start = ((bf16[1,256,5,48]{1,2,0,3:T(8,128)(2,1)}), bf16[1,256,5,48]{1,2,0,3:T(8,128)(2,1)S(1)}, u32[]{:S(2)}, u32[]{:S(2)}) async-start(bf16[1,256,5,48]{1,2,0,3:T(8,128)(2,1)} %copy.56), calls=%async_computation.1 | async-start | bytes 393216 | tf_op jit(solution)/shard_map/all_to_all | solution.py:145
Sparse Core Ops, SparseCore 0:
  14.8 92.8 reduce-scatter.1
  110.0 53.9 all-reduce.3
  165.6 81.0 all-gather.1
where the time goes:
time: 381 us; the launch traced here: 376 us
  waiting for transfers between devices  193 us (51%)
  matrix products  69.5 us (18%)
  blocking collectives  68.2 us (18%)
  other arithmetic  16.9 us (4%)
  between operations  13.9 us (4%)
  local copies, waits for them, and re-layouts  8.04 us (2%)
  starting transfers between devices  6.88 us (2%)
    all_gather x1, waiting for transfers between devices, shards(): whole = lax.all_gather(systems, ('people', 'sub'), axis=1, tiled=True)  81.3 us
    dot_general x10, matrix products, shards(): jnp.dot(system, direction, precision=highest) + shifts * direction  63.4 us
    reduce_scatter x1, waiting for transfers between devices, shards(): lax.psum_scatter(gram_stack, ('people', 'sub'), scatter_dimension=1, tile...  58.8 us
    psum x1, waiting for transfers between devices, shards(): lax.psum((jnp.stack(sums), jnp.stack(squares), jnp.stack(cross), jnp.stac...  44.3 us
    psum x1, blocking collectives, shards(): lax.psum((jnp.stack(sums), jnp.stack(squares), jnp.stack(cross), jnp.stac...  31.6 us
    psum x1, blocking collectives, shards(): gram_two, cross_two = lax.psum((gram_two, cross_two), 'people')  19 us
    all_gather x1, blocking collectives, shards(): lax.all_gather(scaled[None], ('people', 'sub'), axis=0, tiled=True)  17.6 us
  transfers between devices with their start and end apart: 5, of which 5 were waited for; matrix products, arithmetic and copies ran while one was open for 2% of the time, Pallas kernels for 0%

commit v1 on v0

v1 whole, which is shorter than its diff:
```python
import functools

import jax
import jax.numpy as jnp
import numpy as np
from jax import lax
from jax.experimental import pallas as pl
from jax.experimental.pallas import tpu as pltpu
from jax.sharding import PartitionSpec as P

TRAITS = 48
RIDGES = 5
FOLDS = 2
ITERS = 10
ITERS_TWO = 4
AUX = 64
FOLD_ROW = 48
ONE_ROW = 49

MESH = pl.DeviceIdType.MESH
F32 = jnp.float32
BF16 = jnp.bfloat16
NT = (((1,), (1,)), ((), ()))
highest = lax.Precision.HIGHEST


def dot_nt(left, right, precision=None):
    return lax.dot_general(left, right, NT, precision=precision, preferred_element_type=F32)


def kernel(
    sizes,
    dosage, aux, colinfo, perm, ridges,
    out,
    slots, pair, gram, system_hi, system_lo, cross, plain, row_train, row_all, totals, square,
    estimate, residual, direction, split, image, turned, pred, moved, packed, reduced,
    slot_send, slot_recv, forward_send, pair_send, pair_recv,
    pred_send, pred_recv, red_send, red_recv,
):
    depth, lines, share, half, pitch, people = sizes
    rows, block = dosage.shape
    columns = estimate.shape[1]
    train_count = float(people - people // FOLDS)
    z = lax.axis_index("people")
    x = lax.axis_index("blocks")
    core = lax.axis_index("sub")
    other = 1 - core
    total = depth * lines * 2
    me = (z * lines + x) * 2 + core

    barrier = pltpu.get_barrier_semaphore()

    @pl.loop(0, total)
    def _(index):
        @pl.when(index != me)
        def _():
            pl.semaphore_signal(
                barrier, inc=1,
                device_id={
                    "people": index // (lines * 2),
                    "blocks": (index // 2) % lines,
                    "sub": index % 2,
                },
                device_id_type=MESH,
            )

    mine = 2 * z + core
    slots[mine, pl.ds(0, block), :] = (
        jnp.transpose((dosage[...] - 100).astype(F32)).astype(BF16)
    )
    slots[mine, pl.ds(block, AUX), :] = aux[...]
    pair[core] = aux[...]
    pl.semaphore_wait(barrier, total - 1)

    first = depth // 2 - 1
    near = (z >= depth // 2).astype(jnp.int32)

    def slot_copy(place, send_sem, target):
        return pltpu.make_async_remote_copy(
            src_ref=slots.at[place], dst_ref=slots.at[place],
            send_sem=send_sem, recv_sem=slot_recv.at[place],
            device_id=target, device_id_type=MESH,
        )

    for order in range(2):
        goal = first + (near if order == 0 else 1 - near)

        @pl.when(z != goal)
        def _():
            slot_copy(mine, slot_send.at[order], {"people": goal}).start()

    pair_copy = pltpu.make_async_remote_copy(
        src_ref=pair.at[core], dst_ref=pair.at[core],
        send_sem=pair_send, recv_sem=pair_recv,
        device_id={"sub": other}, device_id_type=MESH,
    )
    pair_copy.start()

    solver = z - first
    is_solver = (solver >= 0) & (solver < 2)

    def pred_copy(far, group):
        return pltpu.make_async_remote_copy(
            src_ref=pred.at[far, pl.ds(group * pitch, pitch), :],
            dst_ref=moved.at[x, solver, core],
            send_sem=pred_send.at[far, group],
            recv_sem=pred_recv.at[x, solver, core],
            device_id={"people": far, "blocks": group // 2, "sub": group % 2},
            device_id_type=MESH,
        )

    @pl.when(is_solver)
    def _():
        gram[...] = jnp.zeros_like(gram)
        cross[...] = jnp.zeros_like(cross)
        plain[...] = jnp.zeros_like(plain)
        row_train[...] = jnp.zeros_like(row_train)
        row_all[...] = jnp.zeros_like(row_all)
        totals[...] = jnp.zeros_like(totals)
        square[...] = jnp.zeros_like(square)
        sign = 1 - 2 * solver

        @pl.loop(0, 2 * depth)
        def _(step):
            turn = step // 2
            late = step % 2
            far = z + sign * ((turn + 1) // 2) * (2 * (turn % 2) - 1)
            place = 2 * far + jnp.where(late == 0, core, other)
            copy = slot_copy(place, forward_send.at[far], {"sub": other})

            @pl.when(step > 0)
            def _():
                copy.wait_recv()

            @pl.when(late == 0)
            def _():
                copy.start()

            extra = slots[place, pl.ds(block, AUX), :]
            tail = slots[place, pl.ds(block + FOLD_ROW, AUX - FOLD_ROW), :]
            keep = (tail[0:1, :].astype(F32) != core.astype(F32)).astype(F32).astype(BF16)
            whole = slots[place, pl.ds(0, block), :]
            tile = 256
            for part in range(block // tile):
                span = pl.ds(part * tile, tile)
                own = slots[place, span, :]
                masked = own * keep
                gram[span, :] += dot_nt(masked, whole)
                cross[span, :] += dot_nt(masked, extra)
                plain[span, :] += dot_nt(own, extra)
                row_train[:, span] += dot_nt(tail, masked)
                row_all[:, span] += dot_nt(tail, own)
                wide = own.astype(F32)
                wide = wide * wide
                added = wide[:, 0:128]
                for lane in range(1, rows // 128):
                    added = added + wide[:, lane * 128:(lane + 1) * 128]
                square[span, :] += added
            totals[...] += dot_nt(tail * keep, extra)

        one = ONE_ROW - FOLD_ROW
        mean_row = row_all[one:one + 1, :] / people
        train_row = row_train[one:one + 1, :]
        square_row = dot_nt(jnp.ones((8, 128), F32), square[...], highest)[0:1, :]
        inverse_row = 1.0 / jnp.sqrt(square_row / people - mean_row * mean_row + 1e-05)
        shifted_row = train_row - train_count * mean_row
        pick = (
            lax.broadcasted_iota(jnp.int32, (AUX, columns), 0)
            == colinfo[0:1, :] + solver * half
        ).astype(F32)
        which = colinfo[1:2, :]
        shifts = jnp.zeros((1, columns), F32)
        for ridge in range(RIDGES):
            shifts = shifts + jnp.where(which == ridge, ridges[ridge], 0.0)
        totals_row = jnp.dot(
            totals[...], pick, precision=highest, preferred_element_type=F32
        )[one:one + 1, :]
        tile = 128
        current = jnp.zeros((1, columns), F32)
        for part in range(block // tile):
            span = pl.ds(part * tile, tile)
            mean_col = plain[span, ONE_ROW:ONE_ROW + 1] / people
            train_col = cross[span, ONE_ROW:ONE_ROW + 1]
            square_col = jnp.sum(square[span, :], 1, keepdims=True)
            spread_col = jnp.sqrt(square_col / people - mean_col * mean_col + 1e-05)
            scale_col = 1.0 / (train_count * spread_col)
            value = gram[span, :] - train_col * mean_row - mean_col * shifted_row
            value = value * scale_col * inverse_row
            high = value.astype(BF16)
            system_hi[span, :] = high
            system_lo[span, :] = (value - high.astype(F32)).astype(BF16)
            right = jnp.dot(
                cross[span, :], pick, precision=highest, preferred_element_type=F32
            )
            right = (right - mean_col * totals_row) * scale_col
            residual[span, :] = right
            direction[span, :] = right
            estimate[span, :] = jnp.zeros_like(right)
            high = right.astype(BF16)
            split[span, 0:columns] = high
            split[span, columns:2 * columns] = (right - high.astype(F32)).astype(BF16)
            current = current + jnp.sum(right * right, 0, keepdims=True)

        tile = 256

        def step(_, current):
            both = split[...]
            leading = split[:, 0:columns]
            curve = jnp.zeros((1, columns), F32)
            for part in range(block // tile):
                span = pl.ds(part * tile, tile)
                wide = jnp.dot(system_hi[span, :], both, preferred_element_type=F32)
                narrow = jnp.dot(system_lo[span, :], leading, preferred_element_type=F32)
                along = direction[span, :]
                value = wide[:, 0:columns] + (wide[:, columns:] + narrow) + shifts * along
                image[span, :] = value
                curve = curve + jnp.sum(along * value, 0, keepdims=True)
            alpha = current / curve
            following = jnp.zeros((1, columns), F32)
            for part in range(block // tile):
                span = pl.ds(part * tile, tile)
                estimate[span, :] += alpha * direction[span, :]
                left = residual[span, :] - alpha * image[span, :]
                residual[span, :] = left
                following = following + jnp.sum(left * left, 0, keepdims=True)
            ratio = following / current
            for part in range(block // tile):
                span = pl.ds(part * tile, tile)
                along = residual[span, :] + ratio * direction[span, :]
                direction[span, :] = along
                high = along.astype(BF16)
                split[span, 0:columns] = high
                split[span, columns:2 * columns] = (along - high.astype(F32)).astype(BF16)
            return following

        lax.fori_loop(0, ITERS, step, current)

        for part in range(block // tile):
            span = pl.ds(part * tile, tile)
            mean_col = plain[span, ONE_ROW:ONE_ROW + 1] / people
            square_col = jnp.sum(square[span, :], 1, keepdims=True)
            spread_col = jnp.sqrt(square_col / people - mean_col * mean_col + 1e-05)
            image[span, :] = estimate[span, :] / spread_col
        flipped = jnp.transpose(image[...]).astype(BF16)
        turned[...] = flipped
        offset = jnp.sum(flipped.astype(F32) * mean_row, 1, keepdims=True)

        @pl.loop(0, depth)
        def _(far):
            for side in range(2):
                place = 2 * far + side
                outcome = jnp.dot(
                    turned[...], slots[place, pl.ds(0, block), :], preferred_element_type=F32
                )
                tail = slots[place, pl.ds(block + FOLD_ROW, AUX - FOLD_ROW), :]
                held = tail[0:1, :].astype(F32) == core.astype(F32)
                pred[far, :, side * rows:(side + 1) * rows] = jnp.where(
                    held, outcome - offset, 0.0
                ).astype(BF16)
            for group in range(2 * lines):
                self_here = (far == z) & (x == group // 2) & (core == group % 2)

                @pl.when(self_here)
                def _():
                    moved[x, solver, core] = pred[far, group * pitch:(group + 1) * pitch, :]

                @pl.when(jnp.logical_not(self_here))
                def _():
                    pred_copy(far, group).start()

    pair_copy.wait()
    for line in range(lines):
        for which_solver in range(2):
            for side in range(2):
                self_here = (z == first + which_solver) & (x == line) & (core == side)

                @pl.when(jnp.logical_not(self_here))
                def _():
                    pltpu.make_async_remote_copy(
                        src_ref=moved.at[line, which_solver, side],
                        dst_ref=moved.at[line, which_solver, side],
                        send_sem=red_send.at[0],
                        recv_sem=pred_recv.at[line, which_solver, side],
                        device_id={"sub": other}, device_id_type=MESH,
                    ).wait_recv()

    group = x * 2 + core
    choose = (
        (lax.broadcasted_iota(jnp.int32, (16, AUX), 1)
         == group * share + lax.broadcasted_iota(jnp.int32, (16, AUX), 0))
        & (lax.broadcasted_iota(jnp.int32, (16, AUX), 0) < share)
    ).astype(F32).astype(BF16)
    target = jnp.concatenate(
        [jnp.dot(choose, pair[side], preferred_element_type=F32) for side in range(2)], 1
    )
    predictors = []
    for line in range(lines):
        stacked = jnp.concatenate(
            [moved[line, which, 0] + moved[line, which, 1] for which in range(2)], 0
        )
        ordered = jnp.dot(perm[...], stacked, preferred_element_type=F32)
        for ridge in range(RIDGES):
            predictors.append(ordered[ridge * 16:(ridge + 1) * 16, :])
    count = len(predictors)
    pairs = [(a, b) for a in range(count) for b in range(a, count)]
    width = packed.shape[1]
    lane = lax.broadcasted_iota(jnp.int32, (16, width), 1)
    gathered = jnp.zeros((16, width), F32)
    for index, (a, b) in enumerate(pairs + [(a, None) for a in range(count)]):
        product = predictors[a] * (target if b is None else predictors[b])
        gathered = jnp.where(lane == index, jnp.sum(product, 1, keepdims=True), gathered)
    packed[...] = gathered

    def red_copy(far):
        return pltpu.make_async_remote_copy(
            src_ref=packed, dst_ref=reduced.at[z],
            send_sem=red_send.at[far], recv_sem=red_recv.at[z],
            device_id={"people": far}, device_id_type=MESH,
        )

    reduced[z] = gathered
    for far in range(depth):
        @pl.when(z != far)
        def _():
            red_copy(far).start()
    for far in range(depth):
        @pl.when(z != far)
        def _():
            pltpu.make_async_remote_copy(
                src_ref=packed, dst_ref=reduced.at[far],
                send_sem=red_send.at[far], recv_sem=red_recv.at[far],
                device_id={"people": far}, device_id_type=MESH,
            ).wait_recv()
    summed = reduced[0]
    for far in range(1, depth):
        summed = summed + reduced[far]
    summed = summed / people
    small = {}
    for index, (a, b) in enumerate(pairs):
        small[a, b] = jnp.broadcast_to(summed[:, index:index + 1], (16, 128))
        small[b, a] = small[a, b]
    level = small[0, 0]
    for a in range(1, count):
        level = level + small[a, a]
    level = level / count + 1e-06
    ridge_lane = lax.broadcasted_iota(jnp.int32, (16, 128), 1)
    ridge_row = jnp.zeros((16, 128), F32)
    for ridge in range(RIDGES):
        ridge_row = ridge_row + jnp.where(ridge_lane == ridge, ridges[ridge], 0.0)
    lift = level * ridge_row
    base = len(pairs)
    left = [
        jnp.broadcast_to(summed[:, base + a:base + a + 1], (16, 128)) for a in range(count)
    ]
    along = list(left)
    gamma = [jnp.zeros((16, 128), F32) for _ in range(count)]
    now = sum(v * v for v in left)
    for _ in range(ITERS_TWO):
        result = [
            sum(small[a, b] * along[b] for b in range(count)) + lift * along[a]
            for a in range(count)
        ]
        alpha = now / sum(along[a] * result[a] for a in range(count))
        gamma = [gamma[a] + alpha * along[a] for a in range(count)]
        left = [left[a] - alpha * result[a] for a in range(count)]
        later = sum(v * v for v in left)
        ratio = later / now
        along = [left[a] + ratio * along[a] for a in range(count)]
        now = later
    for ridge in range(RIDGES):
        value = predictors[0] * gamma[0][:, ridge:ridge + 1]
        for a in range(1, count):
            value = value + predictors[a] * gamma[a][:, ridge:ridge + 1]
        out[ridge] = value

    for order in range(2):
        goal = first + (near if order == 0 else 1 - near)

        @pl.when(z != goal)
        def _():
            slot_copy(mine, slot_send.at[order], {"people": goal}).wait_send()

    for far in range(depth):
        @pl.when(z != far)
        def _():
            red_copy(far).wait_send()

    @pl.when(is_solver)
    def _():
        @pl.loop(0, depth)
        def _(far):
            slot_copy(2 * far + core, forward_send.at[far], {"sub": other}).wait_send()
            for group in range(2 * lines):
                self_here = (far == z) & (x == group // 2) & (core == group % 2)

                @pl.when(jnp.logical_not(self_here))
                def _():
                    pred_copy(far, group).wait_send()


def shards(dosage, fold, pheno, ridges):
    rows, block = dosage.shape
    depth = lax.axis_size("people")
    lines = lax.axis_size("blocks")
    people = rows * depth * 2
    groups = lines * 2
    share = TRAITS // groups
    half = share // 2
    pitch = -(-RIDGES * half // 16) * 16
    columns = groups * pitch
    aux = jnp.concatenate(
        [
            pheno.T,
            fold.astype(BF16)[None, :],
            jnp.ones((1, rows), BF16),
            jnp.zeros((AUX - TRAITS - 2, rows), BF16),
        ],
        0,
    )
    info = np.zeros((8, columns), np.int32)
    perm = np.zeros((RIDGES * 16, 2 * pitch), np.float32)
    for group in range(groups):
        for within in range(pitch):
            ridge, local = divmod(within, half) if within < RIDGES * half else (0, 0)
            info[0, group * pitch + within] = group * share + local
            info[1, group * pitch + within] = ridge
    for which in range(2):
        for within in range(RIDGES * half):
            ridge, local = divmod(within, half)
            perm[ridge * 16 + which * half + local, which * pitch + within] = 1.0
    count = lines * RIDGES
    width = -(-(count * (count + 1) // 2 + count) // 128) * 128
    vmem = pl.BlockSpec(memory_space=pltpu.VMEM)
    dma = pltpu.SemaphoreType.DMA
    result = pl.pallas_call(
        functools.partial(kernel, (depth, lines, share, half, pitch, people)),
        out_shape=jax.ShapeDtypeStruct((RIDGES, 16, 2 * rows), F32),
        in_specs=[vmem, vmem, vmem, vmem, pl.BlockSpec(memory_space=pltpu.SMEM)],
        out_specs=vmem,
        scratch_shapes=[
            pltpu.VMEM((2 * depth, block + AUX, rows), BF16),
            pltpu.VMEM((2, AUX, rows), BF16),
            pltpu.VMEM((block, block), F32),
            pltpu.VMEM((block, block), BF16),
            pltpu.VMEM((block, block), BF16),
            pltpu.VMEM((block, AUX), F32),
            pltpu.VMEM((block, AUX), F32),
            pltpu.VMEM((AUX - FOLD_ROW, block), F32),
            pltpu.VMEM((AUX - FOLD_ROW, block), F32),
            pltpu.VMEM((AUX - FOLD_ROW, AUX), F32),
            pltpu.VMEM((block, 128), F32),
            pltpu.VMEM((block, columns), F32),
            pltpu.VMEM((block, columns), F32),
            pltpu.VMEM((block, columns), F32),
            pltpu.VMEM((block, 2 * columns), BF16),
            pltpu.VMEM((block, columns), F32),
            pltpu.VMEM((columns, block), BF16),
            pltpu.VMEM((depth, columns, 2 * rows), BF16),
            pltpu.VMEM((lines, 2, 2, pitch, 2 * rows), BF16),
            pltpu.VMEM((16, width), F32),
            pltpu.VMEM((depth, 16, width), F32),
            dma((2,)),
            dma((2 * depth,)),
            dma((depth,)),
            dma,
            dma,
            dma((depth, groups)),
            dma((lines, 2, 2)),
            dma((depth,)),
            dma((depth,)),
        ],
        compiler_params=pltpu.CompilerParams(
            collective_id=0, has_side_effects=True, vmem_limit_bytes=56 * 1024 * 1024
        ),
    )(dosage, aux, jnp.asarray(info), jnp.asarray(perm, BF16), ridges)
    return jnp.transpose(result[:, :share, :], (1, 0, 2))


def solution(mesh):
    return jax.shard_map(
        shards,
        mesh=mesh,
        in_specs=(
            P(("groups", "people", "sub"), "blocks"),
            P(("groups", "people", "sub")),
            P(("groups", "people", "sub"), None),
            P(),
        ),
        out_specs=P(("blocks", "sub"), None, ("groups", "people")),
        check_vma=False,
    )
```

time: 381 us -> 72.9 us (0.19)
  waiting for transfers between devices: 193 us -> 0 us
  matrix products: 69.5 us -> 0 us
  blocking collectives: 68.2 us -> 0 us
  Pallas kernels: 0 us -> 67.9 us
  other arithmetic: 16.9 us -> 1.44 us
  between operations: 13.9 us -> 0.01 us
  starting transfers between devices: 6.88 us -> 0 us
  local copies, waits for them, and re-layouts: 8.04 us -> 2.44 us
    all_gather x1 -> x0, waiting for transfers between devices: 81.3 us -> none  [shards(): whole = lax.all_gather(systems, ('people', 'sub'), axis=1, tiled=True)]
    dot_general x25 -> x0, matrix products: 69.5 us -> none  [the longest x10 63.4 us: shards(): jnp.dot(system, direction, precision=highest) + shifts * direction]
    pallas_call x0 -> x1, Pallas kernels: none -> 67.9 us  [shards(): pl.pallas_call(functools.partial(kernel, (depth, lines, share, half, pitc...]
    reduce_scatter x1 -> x0, waiting for transfers between devices: 58.8 us -> none  [shards(): lax.psum_scatter(gram_stack, ('people', 'sub'), scatter_dimension=1, tile...]
    psum x2 -> x0, blocking collectives: 50.6 us -> none  [the longest x1 31.6 us: shards(): lax.psum((jnp.stack(sums), jnp.stack(squares), jnp.stack(cross), jnp.stac...]
    psum x1 -> x0, waiting for transfers between devices: 44.3 us -> none  [shards(): lax.psum((jnp.stack(sums), jnp.stack(squares), jnp.stack(cross), jnp.stac...]
    all_gather x1 -> x0, blocking collectives: 17.6 us -> none  [shards(): lax.all_gather(scaled[None], ('people', 'sub'), axis=0, tiled=True)]
    all_to_all x2 -> x0, waiting for transfers between devices: 8.59 us -> none  [the longest x1 5.09 us: shards(): lax.all_to_all(prediction, ('blocks', 'sub'), split_axis=3, concat_axis=0...]
  transfers between devices with their start and end apart: 5 -> 0, of which waited for: 5 -> 0; matrix products, arithmetic and copies ran while one was open for 2% -> 0% of each run, Pallas kernels for 0% -> 0%
where the time goes in v1:
time: 72.9 us; the launch traced here: 71.8 us
  Pallas kernels  67.9 us (93%)
  local copies, waits for them, and re-layouts  2.44 us (3%)
  other arithmetic  1.44 us (2%)
    pallas_call x1, Pallas kernels, shards(): pl.pallas_call(functools.partial(kernel, (depth, lines, share, half, pitc...  67.9 us
    transpose x1, local copies, waits for them, and re-layouts, shards(): return jnp.transpose(result[:, :share, :], (1, 0, 2))  1.59 us

profile of v1, /device:TPU:0, one launch (start us, length us, event | category | flops | bytes accessed | tf_op | source)
XLA Modules:
  0.0 71.8 jit_solution(7677819535686584951)
XLA Ops:
  0.0 0.0 copy-start
  0.0 0.7 copy-done
  0.7 0.1 pad.2.clone
  0.8 0.1 pad.3.clone
  0.8 1.4 %maximum_maximum_fusion.aux = bf16[64,256]{1,0:T(8,128)(2,1)} fusion(bf16[1,256]{1,0:T(2,128)(2,1)S(1)} %broadcast_in_dim.9, bf16[48,256]{1,0:T(8,128)(2,1)} %bitcast.4, bf16[64]{0:T(256)(128)(2,1)S(1)} %pad.3.clone, bf16[64]{0:T(256)(128)(2,1)S(1)} %pad.2.clone), kind=kLoop, calls=%fused_computation.1 | loop fusion | flops 131072 | bytes 58112 | tf_op jit(solution)/shard_map/concatenate | solution.py:411
  2.3 67.9 %shard_map.64 = f32[5,16,512]{2,1,0:T(8,128)} custom-call(s32[256,1024]{1,0:T(8,128)} %dosage.1, bf16[64,256]{1,0:T(8,128)(2,1)} %maximum_maximum_fusion.aux, s32[8,128]{1,0:T(8,128)} %constant.8.clone.colinfo, bf16[80,64]{1,0:T(8,128)(2,1)} %constant.9.clone.perm, f32[5]{0:T(128)} %ridges.1), custom_call_target="tpu_custom_call" | custom-call | tf_op jit(solution)/shard_map/pallas_call | solution.py:435
  70.2 1.6 %slice_bitcast_fusion = f32[12,5,512]{2,0,1:T(8,128)} fusion(f32[5,16,512]{2,1,0:T(8,128)} %shard_map.64), kind=kLoop, calls=%fused_computation | loop fusion | bytes 245760 | tf_op jit(solution)/shard_map/transpose | solution.py:476
  (3 shorter events, 0.0 us)
Async XLA Ops:
  0.0 0.7 copy-start

commit v2 on v1

--- a/solution.py
+++ b/solution.py
@@ -32,7 +32,7 @@
     sizes,
     dosage, aux, colinfo, perm, ridges,
     out,
-    slots, pair, gram, system_hi, system_lo, cross, plain, row_train, row_all, totals, square,
+    slots, pair, gram, system_hi, system_lo, cross, plain, totals, square,
     estimate, residual, direction, split, image, turned, pred, moved, packed, reduced,
     slot_send, slot_recv, forward_send, pair_send, pair_recv,
     pred_send, pred_recv, red_send, red_recv,
@@ -82,19 +82,26 @@
             device_id=target, device_id_type=MESH,
         )
 
-    for order in range(2):
-        goal = first + (near if order == 0 else 1 - near)
-
-        @pl.when(z != goal)
-        def _():
-            slot_copy(mine, slot_send.at[order], {"people": goal}).start()
-
     pair_copy = pltpu.make_async_remote_copy(
         src_ref=pair.at[core], dst_ref=pair.at[core],
         send_sem=pair_send, recv_sem=pair_recv,
         device_id={"sub": other}, device_id_type=MESH,
     )
     pair_copy.start()
+
+    for order in range(2):
+        goal = first + (near if order == 0 else 1 - near)
+
+        if order == 1:
+            closest = first + near
+
+            @pl.when(z != closest)
+            def _():
+                slot_copy(mine, slot_send.at[0], {"people": closest}).wait_send()
+
+        @pl.when(z != goal)
+        def _():
+            slot_copy(mine, slot_send.at[order], {"people": goal}).start()
 
     solver = z - first
     is_solver = (solver >= 0) & (solver < 2)
@@ -114,8 +121,6 @@
         gram[...] = jnp.zeros_like(gram)
         cross[...] = jnp.zeros_like(cross)
         plain[...] = jnp.zeros_like(plain)
-        row_train[...] = jnp.zeros_like(row_train)
-        row_all[...] = jnp.zeros_like(row_all)
         totals[...] = jnp.zeros_like(totals)
         square[...] = jnp.zeros_like(square)
         sign = 1 - 2 * solver
@@ -148,8 +153,6 @@
                 gram[span, :] += dot_nt(masked, whole)
                 cross[span, :] += dot_nt(masked, extra)
                 plain[span, :] += dot_nt(own, extra)
-                row_train[:, span] += dot_nt(tail, masked)
-                row_all[:, span] += dot_nt(tail, own)
                 wide = own.astype(F32)
                 wide = wide * wide
                 added = wide[:, 0:128]
@@ -159,9 +162,20 @@
             totals[...] += dot_nt(tail * keep, extra)
 
         one = ONE_ROW - FOLD_ROW
-        mean_row = row_all[one:one + 1, :] / people
-        train_row = row_train[one:one + 1, :]
-        square_row = dot_nt(jnp.ones((8, 128), F32), square[...], highest)[0:1, :]
+        lane = lax.broadcasted_iota(jnp.int32, (block, 128), 1)
+        table = jnp.where(
+            lane == 0,
+            cross[:, ONE_ROW:ONE_ROW + 1],
+            jnp.where(
+                lane == 1,
+                plain[:, ONE_ROW:ONE_ROW + 1],
+                jnp.sum(square[...], 1, keepdims=True),
+            ),
+        )
+        table = jnp.transpose(table)
+        mean_row = table[1:2, :] / people
+        train_row = table[0:1, :]
+        square_row = table[2:3, :]
         inverse_row = 1.0 / jnp.sqrt(square_row / people - mean_row * mean_row + 1e-05)
         shifted_row = train_row - train_count * mean_row
         pick = (
@@ -196,23 +210,20 @@
             residual[span, :] = right
             direction[span, :] = right
             estimate[span, :] = jnp.zeros_like(right)
-            high = right.astype(BF16)
-            split[span, 0:columns] = high
-            split[span, columns:2 * columns] = (right - high.astype(F32)).astype(BF16)
+            split[span, :] = right.astype(BF16)
             current = current + jnp.sum(right * right, 0, keepdims=True)
 
         tile = 256
 
         def step(_, current):
-            both = split[...]
-            leading = split[:, 0:columns]
+            leading = split[...]
             curve = jnp.zeros((1, columns), F32)
             for part in range(block // tile):
                 span = pl.ds(part * tile, tile)
-                wide = jnp.dot(system_hi[span, :], both, preferred_element_type=F32)
+                wide = jnp.dot(system_hi[span, :], leading, preferred_element_type=F32)
                 narrow = jnp.dot(system_lo[span, :], leading, preferred_element_type=F32)
                 along = direction[span, :]
-                value = wide[:, 0:columns] + (wide[:, columns:] + narrow) + shifts * along
+                value = wide + narrow + shifts * along
                 image[span, :] = value
                 curve = curve + jnp.sum(along * value, 0, keepdims=True)
             alpha = current / curve
@@ -228,9 +239,7 @@
                 span = pl.ds(part * tile, tile)
                 along = residual[span, :] + ratio * direction[span, :]
                 direction[span, :] = along
-                high = along.astype(BF16)
-                split[span, 0:columns] = high
-                split[span, columns:2 * columns] = (along - high.astype(F32)).astype(BF16)
+                split[span, :] = along.astype(BF16)
             return following
 
         lax.fori_loop(0, ITERS, step, current)
@@ -373,12 +382,11 @@
             value = value + predictors[a] * gamma[a][:, ridge:ridge + 1]
         out[ridge] = value
 
-    for order in range(2):
-        goal = first + (near if order == 0 else 1 - near)
-
-        @pl.when(z != goal)
-        def _():
-            slot_copy(mine, slot_send.at[order], {"people": goal}).wait_send()
+    furthest = first + 1 - near
+
+    @pl.when(z != furthest)
+    def _():
+        slot_copy(mine, slot_send.at[1], {"people": furthest}).wait_send()
 
     for far in range(depth):
         @pl.when(z != far)
@@ -445,14 +453,12 @@
             pltpu.VMEM((block, block), BF16),
             pltpu.VMEM((block, AUX), F32),
             pltpu.VMEM((block, AUX), F32),
-            pltpu.VMEM((AUX - FOLD_ROW, block), F32),
-            pltpu.VMEM((AUX - FOLD_ROW, block), F32),
             pltpu.VMEM((AUX - FOLD_ROW, AUX), F32),
             pltpu.VMEM((block, 128), F32),
             pltpu.VMEM((block, columns), F32),
             pltpu.VMEM((block, columns), F32),
             pltpu.VMEM((block, columns), F32),
-            pltpu.VMEM((block, 2 * columns), BF16),
+            pltpu.VMEM((block, columns), BF16),
             pltpu.VMEM((block, columns), F32),
             pltpu.VMEM((columns, block), BF16),
             pltpu.VMEM((depth, columns, 2 * rows), BF16),

time: 72.9 us -> 71.6 us (0.982)
  Pallas kernels: 67.9 us -> 66.7 us
    pallas_call x1, Pallas kernels: 67.9 us -> 66.7 us  [shards(): pl.pallas_call(functools.partial(kernel, (depth, lines, share, half, pitc...]
where the time goes in v2:
time: 71.6 us; the launch traced here: 70.6 us
  Pallas kernels  66.7 us (93%)
  local copies, waits for them, and re-layouts  2.44 us (3%)
  other arithmetic  1.44 us (2%)
    pallas_call x1, Pallas kernels, shards(): pl.pallas_call(functools.partial(kernel, (depth, lines, share, half, pitc...  66.7 us
    transpose x1, local copies, waits for them, and re-layouts, shards(): return jnp.transpose(result[:, :share, :], (1, 0, 2))  1.59 us
    concatenate x1, other arithmetic, shards(): jnp.concatenate([pheno.T, fold.astype(BF16)[None, :], jnp.ones((1, rows),...  1.44 us

profile of v2, /device:TPU:0, one launch (start us, length us, event | category | flops | bytes accessed | tf_op | source)
XLA Modules:
  0.0 70.6 jit_solution(936445505898515901)
XLA Ops:
  0.0 0.0 copy-start
  0.0 0.7 copy-done
  0.7 0.1 pad.2.clone
  0.8 0.1 pad.3.clone
  0.8 1.4 %maximum_maximum_fusion.aux = bf16[64,256]{1,0:T(8,128)(2,1)} fusion(bf16[1,256]{1,0:T(2,128)(2,1)S(1)} %broadcast_in_dim.9, bf16[48,256]{1,0:T(8,128)(2,1)} %bitcast.4, bf16[64]{0:T(256)(128)(2,1)S(1)} %pad.3.clone, bf16[64]{0:T(256)(128)(2,1)S(1)} %pad.2.clone), kind=kLoop, calls=%fused_computation.1 | loop fusion | flops 131072 | bytes 58112 | tf_op jit(solution)/shard_map/concatenate | solution.py:419
  2.3 66.7 %shard_map.64 = f32[5,16,512]{2,1,0:T(8,128)} custom-call(s32[256,1024]{1,0:T(8,128)} %dosage.1, bf16[64,256]{1,0:T(8,128)(2,1)} %maximum_maximum_fusion.aux, s32[8,128]{1,0:T(8,128)} %constant.8.clone.colinfo, bf16[80,64]{1,0:T(8,128)(2,1)} %constant.9.clone.perm, f32[5]{0:T(128)} %ridges.1), custom_call_target="tpu_custom_call" | custom-call | tf_op jit(solution)/shard_map/pallas_call | solution.py:443
  69.0 1.6 %slice_bitcast_fusion = f32[12,5,512]{2,0,1:T(8,128)} fusion(f32[5,16,512]{2,1,0:T(8,128)} %shard_map.64), kind=kLoop, calls=%fused_computation | loop fusion | bytes 245760 | tf_op jit(solution)/shard_map/transpose | solution.py:482
  (3 shorter events, 0.0 us)
Async XLA Ops:
  0.0 0.7 copy-start

commit v3 on v2

--- a/solution.py
+++ b/solution.py
@@ -13,6 +13,7 @@
 FOLDS = 2
 ITERS = 10
 ITERS_TWO = 4
+EXACT = 4
 AUX = 64
 FOLD_ROW = 48
 ONE_ROW = 49
@@ -30,9 +31,9 @@
 
 def kernel(
     sizes,
-    dosage, aux, colinfo, perm, ridges,
+    dosage, fold, pheno, colinfo, perm, ridges,
     out,
-    slots, pair, gram, system_hi, system_lo, cross, plain, totals, square,
+    slots, wide_pheno, pair, gram, system_hi, system_lo, cross, plain, totals, square,
     estimate, residual, direction, split, image, turned, pred, moved, packed, reduced,
     slot_send, slot_recv, forward_send, pair_send, pair_recv,
     pred_send, pred_recv, red_send, red_recv,
@@ -68,8 +69,16 @@
     slots[mine, pl.ds(0, block), :] = (
         jnp.transpose((dosage[...] - 100).astype(F32)).astype(BF16)
     )
-    slots[mine, pl.ds(block, AUX), :] = aux[...]
-    pair[core] = aux[...]
+    wide_pheno[...] = jnp.zeros_like(wide_pheno)
+    wide_pheno[:, 0:TRAITS] = pheno[...].astype(F32)
+    row = lax.broadcasted_iota(jnp.int32, (AUX, rows), 0)
+    aux = jnp.where(
+        row == FOLD_ROW,
+        fold[...].astype(F32),
+        jnp.where(row == ONE_ROW, 1.0, jnp.transpose(wide_pheno[...])[0:AUX, :]),
+    ).astype(BF16)
+    slots[mine, pl.ds(block, AUX), :] = aux
+    pair[core] = aux
     pl.semaphore_wait(barrier, total - 1)
 
     first = depth // 2 - 1
@@ -210,39 +219,51 @@
             residual[span, :] = right
             direction[span, :] = right
             estimate[span, :] = jnp.zeros_like(right)
-            split[span, :] = right.astype(BF16)
+            high = right.astype(BF16)
+            split[span, 0:columns] = high
+            split[span, columns:2 * columns] = (right - high.astype(F32)).astype(BF16)
             current = current + jnp.sum(right * right, 0, keepdims=True)
 
         tile = 256
 
-        def step(_, current):
-            leading = split[...]
+        def step(exact, _, current):
+            both = split[...] if exact else None
+            leading = split[:, 0:columns]
             curve = jnp.zeros((1, columns), F32)
             for part in range(block // tile):
                 span = pl.ds(part * tile, tile)
-                wide = jnp.dot(system_hi[span, :], leading, preferred_element_type=F32)
-                narrow = jnp.dot(system_lo[span, :], leading, preferred_element_type=F32)
                 along = direction[span, :]
-                value = wide + narrow + shifts * along
+                if exact:
+                    wide = jnp.dot(system_hi[span, :], both, preferred_element_type=F32)
+                    narrow = jnp.dot(system_lo[span, :], leading, preferred_element_type=F32)
+                    value = wide[:, 0:columns] + (wide[:, columns:] + narrow)
+                else:
+                    value = jnp.dot(system_hi[span, :], leading, preferred_element_type=F32)
+                value = value + shifts * along
                 image[span, :] = value
                 curve = curve + jnp.sum(along * value, 0, keepdims=True)
             alpha = current / curve
             following = jnp.zeros((1, columns), F32)
             for part in range(block // tile):
                 span = pl.ds(part * tile, tile)
-                estimate[span, :] += alpha * direction[span, :]
                 left = residual[span, :] - alpha * image[span, :]
                 residual[span, :] = left
                 following = following + jnp.sum(left * left, 0, keepdims=True)
             ratio = following / current
             for part in range(block // tile):
                 span = pl.ds(part * tile, tile)
-                along = residual[span, :] + ratio * direction[span, :]
+                along = direction[span, :]
+                estimate[span, :] += alpha * along
+                along = residual[span, :] + ratio * along
                 direction[span, :] = along
-                split[span, :] = along.astype(BF16)
+                high = along.astype(BF16)
+                split[span, 0:columns] = high
+                if exact:
+                    split[span, columns:2 * columns] = (along - high.astype(F32)).astype(BF16)
             return following
 
-        lax.fori_loop(0, ITERS, step, current)
+        current = lax.fori_loop(0, EXACT, functools.partial(step, True), current)
+        lax.fori_loop(EXACT, ITERS, functools.partial(step, False), current)
 
         for part in range(block // tile):
             span = pl.ds(part * tile, tile)
@@ -416,15 +437,6 @@
     half = share // 2
     pitch = -(-RIDGES * half // 16) * 16
     columns = groups * pitch
-    aux = jnp.concatenate(
-        [
-            pheno.T,
-            fold.astype(BF16)[None, :],
-            jnp.ones((1, rows), BF16),
-            jnp.zeros((AUX - TRAITS - 2, rows), BF16),
-        ],
-        0,
-    )
     info = np.zeros((8, columns), np.int32)
     perm = np.zeros((RIDGES * 16, 2 * pitch), np.float32)
     for group in range(groups):
@@ -443,10 +455,11 @@
     result = pl.pallas_call(
         functools.partial(kernel, (depth, lines, share, half, pitch, people)),
         out_shape=jax.ShapeDtypeStruct((RIDGES, 16, 2 * rows), F32),
-        in_specs=[vmem, vmem, vmem, vmem, pl.BlockSpec(memory_space=pltpu.SMEM)],
+        in_specs=[vmem, vmem, vmem, vmem, vmem, pl.BlockSpec(memory_space=pltpu.SMEM)],
         out_specs=vmem,
         scratch_shapes=[
             pltpu.VMEM((2 * depth, block + AUX, rows), BF16),
+            pltpu.VMEM((rows, 128), F32),
             pltpu.VMEM((2, AUX, rows), BF16),
             pltpu.VMEM((block, block), F32),
             pltpu.VMEM((block, block), BF16),
@@ -458,7 +471,7 @@
             pltpu.VMEM((block, columns), F32),
             pltpu.VMEM((block, columns), F32),
             pltpu.VMEM((block, columns), F32),
-            pltpu.VMEM((block, columns), BF16),
+            pltpu.VMEM((block, 2 * columns), BF16),
             pltpu.VMEM((block, columns), F32),
             pltpu.VMEM((columns, block), BF16),
             pltpu.VMEM((depth, columns, 2 * rows), BF16),
@@ -478,7 +491,7 @@
         compiler_params=pltpu.CompilerParams(
             collective_id=0, has_side_effects=True, vmem_limit_bytes=56 * 1024 * 1024
         ),
-    )(dosage, aux, jnp.asarray(info), jnp.asarray(perm, BF16), ridges)
+    )(dosage, fold[None, :], pheno, jnp.asarray(info), jnp.asarray(perm, BF16), ridges)
     return jnp.transpose(result[:, :share, :], (1, 0, 2))
 
 

time: 71.6 us -> 67.7 us (0.946)
  Pallas kernels: 66.7 us -> 63.7 us
  other arithmetic: 1.44 us -> 0 us
    pallas_call x1, Pallas kernels: 66.7 us -> 63.7 us  [shards(): pl.pallas_call(functools.partial(kernel, (depth, lines, share, half, pitc...]
    concatenate x1 -> x0, other arithmetic: 1.44 us -> none  [shards(): jnp.concatenate([pheno.T, fold.astype(BF16)[None, :], jnp.ones((1, rows),...]
    unnamed x2 -> x1, local copies, waits for them, and re-layouts: 0.68 us -> 1.47 us
where the time goes in v3:
time: 67.7 us; the launch traced here: 66.8 us
  Pallas kernels  63.7 us (94%)
  local copies, waits for them, and re-layouts  3.06 us (5%)
    pallas_call x1, Pallas kernels, shards(): pl.pallas_call(functools.partial(kernel, (depth, lines, share, half, pitc...  63.7 us
    transpose x1, local copies, waits for them, and re-layouts, shards(): return jnp.transpose(result[:, :share, :], (1, 0, 2))  1.59 us
    unnamed x1, local copies, waits for them, and re-layouts  1.47 us

profile of v3, /device:TPU:0, one launch (start us, length us, event | category | flops | bytes accessed | tf_op | source)
XLA Modules:
  0.0 66.8 jit_solution(11779533077884681417)
XLA Ops:
  0.0 1.5 %copy.7.pheno = bf16[256,48]{1,0:T(8,128)(2,1)} copy(bf16[256,48]{0,1:T(8,128)(2,1)} %param.8) | data formatting | bytes 49152 | tf_op args[2]
  1.5 63.7 %shard_map.64 = f32[5,16,512]{2,1,0:T(8,128)} custom-call(s32[256,1024]{1,0:T(8,128)} %dosage.1, s32[1,256]{1,0:T(1,128)} %bitcast.3, bf16[256,48]{1,0:T(8,128)(2,1)} %copy.7.pheno, s32[8,128]{1,0:T(8,128)} %constant.4.clone.colinfo, bf16[80,64]{1,0:T(8,128)(2,1)} %constant.5.clone.perm, f32[5]{0:T(128)} %ridges.1), custom_call_target="tpu_custom_call" | custom-call | tf_op jit(solution)/shard_map/pallas_call | solution.py:455
  65.2 1.6 %slice_bitcast_fusion = f32[12,5,512]{2,0,1:T(8,128)} fusion(f32[5,16,512]{2,1,0:T(8,128)} %shard_map.64), kind=kLoop, calls=%fused_computation | loop fusion | bytes 245760 | tf_op jit(solution)/shard_map/transpose | solution.py:495

commit v4 on v3

--- a/solution.py
+++ b/solution.py
@@ -14,6 +14,7 @@
 ITERS = 10
 ITERS_TWO = 4
 EXACT = 4
+PIECES = 4
 AUX = 64
 FOLD_ROW = 48
 ONE_ROW = 49
@@ -84,12 +85,20 @@
     first = depth // 2 - 1
     near = (z >= depth // 2).astype(jnp.int32)
 
-    def slot_copy(place, send_sem, target):
-        return pltpu.make_async_remote_copy(
-            src_ref=slots.at[place], dst_ref=slots.at[place],
-            send_sem=send_sem, recv_sem=slot_recv.at[place],
-            device_id=target, device_id_type=MESH,
-        )
+    stretch = (block + AUX) // PIECES
+
+    def slot_copies(place, send_sem, target):
+        copies = []
+        for piece in range(PIECES):
+            part = slots.at[place, pl.ds(piece * stretch, stretch), :]
+            copies.append(
+                pltpu.make_async_remote_copy(
+                    src_ref=part, dst_ref=part,
+                    send_sem=send_sem.at[piece], recv_sem=slot_recv.at[place, piece],
+                    device_id=target, device_id_type=MESH,
+                )
+            )
+        return copies
 
     pair_copy = pltpu.make_async_remote_copy(
         src_ref=pair.at[core], dst_ref=pair.at[core],
@@ -106,11 +115,13 @@
 
             @pl.when(z != closest)
             def _():
-                slot_copy(mine, slot_send.at[0], {"people": closest}).wait_send()
+                for copy in slot_copies(mine, slot_send.at[0], {"people": closest}):
+                    copy.wait_send()
 
         @pl.when(z != goal)
         def _():
-            slot_copy(mine, slot_send.at[order], {"people": goal}).start()
+            for copy in slot_copies(mine, slot_send.at[order], {"people": goal}):
+                copy.start()
 
     solver = z - first
     is_solver = (solver >= 0) & (solver < 2)
@@ -140,15 +151,15 @@
             late = step % 2
             far = z + sign * ((turn + 1) // 2) * (2 * (turn % 2) - 1)
             place = 2 * far + jnp.where(late == 0, core, other)
-            copy = slot_copy(place, forward_send.at[far], {"sub": other})
-
-            @pl.when(step > 0)
-            def _():
-                copy.wait_recv()
-
-            @pl.when(late == 0)
-            def _():
-                copy.start()
+            for copy in slot_copies(place, forward_send.at[far], {"sub": other}):
+
+                @pl.when(step > 0)
+                def _():
+                    copy.wait_recv()
+
+                @pl.when(late == 0)
+                def _():
+                    copy.start()
 
             extra = slots[place, pl.ds(block, AUX), :]
             tail = slots[place, pl.ds(block + FOLD_ROW, AUX - FOLD_ROW), :]
@@ -276,7 +287,8 @@
         offset = jnp.sum(flipped.astype(F32) * mean_row, 1, keepdims=True)
 
         @pl.loop(0, depth)
-        def _(far):
+        def _(turn):
+            far = jnp.where(solver == 0, depth - 1 - turn, turn)
             for side in range(2):
                 place = 2 * far + side
                 outcome = jnp.dot(
@@ -407,7 +419,8 @@
 
     @pl.when(z != furthest)
     def _():
-        slot_copy(mine, slot_send.at[1], {"people": furthest}).wait_send()
+        for copy in slot_copies(mine, slot_send.at[1], {"people": furthest}):
+            copy.wait_send()
 
     for far in range(depth):
         @pl.when(z != far)
@@ -418,7 +431,8 @@
     def _():
         @pl.loop(0, depth)
         def _(far):
-            slot_copy(2 * far + core, forward_send.at[far], {"sub": other}).wait_send()
+            for copy in slot_copies(2 * far + core, forward_send.at[far], {"sub": other}):
+                copy.wait_send()
             for group in range(2 * lines):
                 self_here = (far == z) & (x == group // 2) & (core == group % 2)
 
@@ -478,9 +492,9 @@
             pltpu.VMEM((lines, 2, 2, pitch, 2 * rows), BF16),
             pltpu.VMEM((16, width), F32),
             pltpu.VMEM((depth, 16, width), F32),
-            dma((2,)),
-            dma((2 * depth,)),
-            dma((depth,)),
+            dma((2, PIECES)),
+            dma((2 * depth, PIECES)),
+            dma((depth, PIECES)),
             dma,
             dma,
             dma((depth, groups)),

time: 67.7 us -> 66 us (0.975); the launches traced: 66.8 us -> 65.8 us
  Pallas kernels: 63.7 us -> 62.7 us
    pallas_call x1, Pallas kernels: 63.7 us -> 62.7 us  [shards(): pl.pallas_call(functools.partial(kernel, (depth, lines, share, half, pitc...]
where the time goes in v4:
time: 66 us; the launch traced here: 65.8 us
  Pallas kernels  62.7 us (95%)
  local copies, waits for them, and re-layouts  3.06 us (5%)
    pallas_call x1, Pallas kernels, shards(): pl.pallas_call(functools.partial(kernel, (depth, lines, share, half, pitc...  62.7 us
    transpose x1, local copies, waits for them, and re-layouts, shards(): return jnp.transpose(result[:, :share, :], (1, 0, 2))  1.59 us
    unnamed x1, local copies, waits for them, and re-layouts  1.47 us

profile of v4, /device:TPU:0, one launch (start us, length us, event | category | flops | bytes accessed | tf_op | source)
XLA Modules:
  0.0 65.8 jit_solution(6060643381730824618)
XLA Ops:
  0.0 1.5 %copy.7.pheno = bf16[256,48]{1,0:T(8,128)(2,1)} copy(bf16[256,48]{0,1:T(8,128)(2,1)} %param.8) | data formatting | bytes 49152 | tf_op args[2]
  1.5 62.7 %shard_map.64 = f32[5,16,512]{2,1,0:T(8,128)} custom-call(s32[256,1024]{1,0:T(8,128)} %dosage.1, s32[1,256]{1,0:T(1,128)} %bitcast.3, bf16[256,48]{1,0:T(8,128)(2,1)} %copy.7.pheno, s32[8,128]{1,0:T(8,128)} %constant.4.clone.colinfo, bf16[80,64]{1,0:T(8,128)(2,1)} %constant.5.clone.perm, f32[5]{0:T(128)} %ridges.1), custom_call_target="tpu_custom_call" | custom-call | tf_op jit(solution)/shard_map/pallas_call | solution.py:469
  64.2 1.6 %slice_bitcast_fusion = f32[12,5,512]{2,0,1:T(8,128)} fusion(f32[5,16,512]{2,1,0:T(8,128)} %shard_map.64), kind=kLoop, calls=%fused_computation | loop fusion | bytes 245760 | tf_op jit(solution)/shard_map/transpose | solution.py:509

commit v5 on v4

--- a/solution.py
+++ b/solution.py
@@ -235,7 +235,7 @@
             split[span, columns:2 * columns] = (right - high.astype(F32)).astype(BF16)
             current = current + jnp.sum(right * right, 0, keepdims=True)
 
-        tile = 256
+        tile = block // 2
 
         def step(exact, _, current):
             both = split[...] if exact else None

time: 66 us -> 67.1 us (1.017)
  Pallas kernels: 62.7 us -> 63.8 us
    pallas_call x1, Pallas kernels: 62.7 us -> 63.8 us  [shards(): pl.pallas_call(functools.partial(kernel, (depth, lines, share, half, pitc...]
where the time goes in v5:
time: 67.1 us; the launch traced here: 66.9 us
  Pallas kernels  63.8 us (95%)
  local copies, waits for them, and re-layouts  3.06 us (5%)
    pallas_call x1, Pallas kernels, shards(): pl.pallas_call(functools.partial(kernel, (depth, lines, share, half, pitc...  63.8 us
    transpose x1, local copies, waits for them, and re-layouts, shards(): return jnp.transpose(result[:, :share, :], (1, 0, 2))  1.59 us
    unnamed x1, local copies, waits for them, and re-layouts  1.47 us

profile of v5, /device:TPU:0, one launch (start us, length us, event | category | flops | bytes accessed | tf_op | source)
XLA Modules:
  0.0 66.9 jit_solution(7572716263165786959)
XLA Ops:
  0.0 1.5 %copy.7.pheno = bf16[256,48]{1,0:T(8,128)(2,1)} copy(bf16[256,48]{0,1:T(8,128)(2,1)} %param.8) | data formatting | bytes 49152 | tf_op args[2]
  1.5 63.8 %shard_map.64 = f32[5,16,512]{2,1,0:T(8,128)} custom-call(s32[256,1024]{1,0:T(8,128)} %dosage.1, s32[1,256]{1,0:T(1,128)} %bitcast.3, bf16[256,48]{1,0:T(8,128)(2,1)} %copy.7.pheno, s32[8,128]{1,0:T(8,128)} %constant.4.clone.colinfo, bf16[80,64]{1,0:T(8,128)(2,1)} %constant.5.clone.perm, f32[5]{0:T(128)} %ridges.1), custom_call_target="tpu_custom_call" | custom-call | tf_op jit(solution)/shard_map/pallas_call | solution.py:469
  65.3 1.6 %slice_bitcast_fusion = f32[12,5,512]{2,0,1:T(8,128)} fusion(f32[5,16,512]{2,1,0:T(8,128)} %shard_map.64), kind=kLoop, calls=%fused_computation | loop fusion | bytes 245760 | tf_op jit(solution)/shard_map/transpose | solution.py:509
